TPU v7x, 32 devices: a whole 2x2x4 slice. The times are simulated.
32 devices in a mesh: row: 8 (over z, y), col: 4 (over x, core).
Axes of the slice: x: 2, y: 2, z: 4, core: 2. Of those that a mesh axis runs over, the one named last changes fastest.
Arguments:
- a_slab: float32 [4096, 1024], P('row', 'col'), may hold values from -6 to 6
- b_panel: float32 [1024, 16384], P('row', 'col'), may hold values from -0.1875 to 0.1875
- row_weights: float32 [2, 4096], P(None, 'row'), may hold values from -0.09375 to 0.09375
- col_weights: float32 [2, 16384], P(None, 'col'), may hold values from -0.046875 to 0.046875
Outputs:
- product: float32 [4096, 16384], P('row', 'col')
- check_rows: float32 [2, 16384], P(None, 'col')
- check_cols: float32 [2, 4096], P(None, 'row')
All inputs are finite; a program needn't handle non-finite values.
Results may differ from a plain program's by a relative error of at most 0.000076.
Values sent between devices are 32-bit elements; how exact they have to be, the bound alone decides.
A program may use at most 64 MiB of HBM per device.

v0:
```python
import jax
import jax.numpy as jnp
from jax import lax
from jax.sharding import PartitionSpec as P


def dot(left, right, dims):
    return lax.dot_general(
        left, right, (dims, ((), ())), precision=lax.Precision.HIGH, preferred_element_type=jnp.float32
    )


def per_device(a_slab, b_panel, row_weights, col_weights):
    b_whole = lax.all_gather(b_panel, "row", axis=0, tiled=True)
    a_whole = lax.all_gather(a_slab, "col", axis=1, tiled=True)
    a_part = lax.psum(dot(row_weights, a_slab, ((1,), (0,))), "row")
    a_check = lax.all_gather(a_part, "col", axis=1, tiled=True)
    b_part = lax.psum(dot(col_weights, b_panel, ((1,), (1,))), "col")
    b_check = lax.all_gather(b_part, "row", axis=1, tiled=True)
    check_cols = dot(b_check, a_whole, ((1,), (1,)))
    product = dot(a_whole, b_whole, ((1,), (0,)))
    check_rows = dot(a_check, b_whole, ((1,), (0,)))
    return (product, check_rows, check_cols)


def solution(mesh):
    placed = (P("row", "col"), P("row", "col"), P(None, "row"), P(None, "col"))
    return jax.shard_map(
        per_device,
        mesh=mesh,
        in_specs=placed,
        out_specs=(P("row", "col"), P(None, "col"), P(None, "row")),
        check_vma=False,
    )
```

profile of v0, /device:TPU:0, one launch (start us, length us, event | category | flops | bytes accessed | tf_op | source)
XLA Modules:
  0.0 296.4 jit_solution(16877034660809632944)
XLA Ops:
  7.2 0.0 copy-start
  7.2 0.0 copy-start.2
  7.2 0.0 all-gather.3.cloned.1.call-start
  7.2 0.7 all-gather.3.cloned.1.call-update
  7.9 0.0 copy-start.4
  7.9 0.0 copy-start.5
  7.9 0.0 all-gather.5.cloned.1.call-start
  8.0 0.7 all-gather.5.cloned.1.call-update
  8.7 0.0 copy-done
  8.7 0.1 copy-done.2
  8.8 0.9 fusion.3
  9.7 8.3 %psum.15 = f32[2,128]{1,0:T(2,128)S(1)} all-reduce(f32[2,128]{1,0:T(2,128)S(1)} %fusion.3), channel_id=1, replica_groups=mesh['row'=8,'col'=4] {'col'}, use_global_device_ids=true, to_apply=%region_1.0 | all-reduce | flops 256 | bytes 2048 | tf_op jit(solution)/shard_map/psum | solution.py:18
  18.0 0.0 copy-done.4
  18.0 0.0 copy-done.5
  18.0 0.2 fusion.1
  18.2 21.7 %psum.14 = f32[2,256]{1,0:T(2,128)S(1)} all-reduce(f32[2,256]{1,0:T(2,128)S(1)} %fusion.1), channel_id=1, replica_groups=mesh['row'=8,'col'=4] {'row'}, use_global_device_ids=true, to_apply=%region_0.0 | all-reduce | flops 512 | bytes 4096 | tf_op jit(solution)/shard_map/psum | solution.py:16
  39.9 5.1 %all_gather.14 = f32[2,1024]{1,0:T(2,128)S(1)} all-gather(f32[2,256]{1,0:T(2,128)S(1)} %psum.14), channel_id=1, replica_groups=mesh['row'=8,'col'=4] {'col'}, dimensions={1}, use_global_device_ids=true | all-gather | bytes 10240 | tf_op jit(solution)/shard_map/all_gather | solution.py:17
  45.1 16.5 %all_gather.15 = f32[2,1024]{1,0:T(2,128)S(1)} all-gather(f32[2,128]{1,0:T(2,128)S(1)} %psum.15), channel_id=1, replica_groups=mesh['row'=8,'col'=4] {'row'}, dimensions={1}, use_global_device_ids=true | all-gather | bytes 9216 | tf_op jit(solution)/shard_map/all_gather | solution.py:19
  61.6 0.0 all-gather.3.cloned.1.call-done
  61.6 0.0 copy-start.3
  61.6 3.3 %fusion.4 = f32[2,512]{1,0:T(2,128)} fusion(f32[2,1024]{1,0:T(2,128)S(1)} %all_gather.15, f32[512,1024]{1,0:T(8,128)} %all-gather.3.cloned.1.call-done), kind=kOutput, calls=%fused_computation.4 | convolution fusion | flops 6291456 | bytes 2109440 | tf_op jit(solution)/shard_map/dot_general | solution.py:8
  64.9 199.8 %all-gather.5.cloned.1.call-done = f32[1024,4096]{1,0:T(8,128)} async-done(((f32[128,4096]{1,0:T(8,128)}), f32[1024,4096]{1,0:T(8,128)}) %all-gather.5.cloned.1.call-update) | async-done | bytes 16777232 | tf_op jit(solution)/shard_map/all_gather | solution.py:14
  264.7 0.0 copy-done.3
  264.7 0.0 copy-start.1
  264.7 19.4 %fusion = f32[512,4096]{1,0:T(8,128)} fusion(f32[512,1024]{1,0:T(8,128)S(1)} %copy-done.3, f32[1024,4096]{1,0:T(8,128)} %all-gather.5.cloned.1.call-done), kind=kOutput, calls=%fused_computation | convolution fusion | flops 12884901888 | bytes 27262976 | tf_op jit(solution)/shard_map/dot_general | solution.py:8
  284.1 0.0 copy-done.1
  284.1 5.5 %fusion.2 = f32[2,4096]{1,0:T(2,128)} fusion(f32[2,1024]{1,0:T(2,128)S(1)} %all_gather.14, f32[1024,4096]{1,0:T(8,128)S(1)} %copy-done.1), kind=kOutput, calls=%fused_computation.2 | convolution fusion | flops 50331648 | bytes 16818176 | tf_op jit(solution)/shard_map/dot_general | solution.py:8
Async XLA Ops:
  7.2 1.5 copy-start
  7.2 1.6 copy-start.2
  7.2 54.4 %all-gather.3.cloned.1.call-start = ((), (), s32[]{:S(2)}) async-start(), calls=%async_computation | async-start | bytes 2621440 | tf_op jit(solution)/shard_map/all_gather | solution.py:15
  7.9 10.1 %copy-start.4 = (f32[512,256]{1,0:T(8,128)S(1)}, f32[512,256]{1,0:T(8,128)}, u32[]{:S(2)}) copy-start(f32[512,256]{1,0:T(8,128)} %param.4) | copy-start | bytes 1572868
  7.9 10.1 %copy-start.5 = (f32[2,512]{1,0:T(2,128)S(1)}, f32[2,512]{1,0:T(2,128)}, u32[]{:S(2)}) copy-start(f32[2,512]{1,0:T(2,128)} %param.6) | copy-start | bytes 12292
  7.9 256.7 %all-gather.5.cloned.1.call-start = ((), (), s32[]{:S(2)}) async-start(), calls=%async_computation.1 | async-start | bytes 18874368 | tf_op jit(solution)/shard_map/all_gather | solution.py:14
  61.6 203.1 %copy-start.3 = (f32[512,1024]{1,0:T(8,128)S(1)}, f32[512,1024]{1,0:T(8,128)}, u32[]{:S(2)}) copy-start(f32[512,1024]{1,0:T(8,128)} %all-gather.3.cloned.1.call-done) | copy-start | bytes 6291460
  264.7 19.4 %copy-start.1 = (f32[1024,4096]{1,0:T(8,128)S(1)}, f32[1024,4096]{1,0:T(8,128)}, u32[]{:S(2)}) copy-start(f32[1024,4096]{1,0:T(8,128)} %all-gather.5.cloned.1.call-done) | copy-start | bytes 50331652
Sparse Core Ops, SparseCore 0:
  9.6 25.2 all-gather.2
  37.0 227.6 all-gather.4
where the time goes:
time: 297 us; the launch traced here: 296 us
  waiting for transfers between devices  201 us (68%)
  blocking collectives  51.7 us (17%)
  matrix products  29.3 us (10%)
  between operations  14.1 us (5%)
    all_gather x1, waiting for transfers between devices, per_device(): b_whole = lax.all_gather(b_panel, 'row', axis=0, tiled=True)  200 us
    dot_general x5, matrix products, dot(): lax.dot_general(left, right, (dims, ((), ())), precision=lax.Precision.HI...  29.3 us
    psum x1, blocking collectives, per_device(): a_part = lax.psum(dot(row_weights, a_slab, ((1,), (0,))), 'row')  21.7 us
    all_gather x1, blocking collectives, per_device(): b_check = lax.all_gather(b_part, 'row', axis=1, tiled=True)  16.5 us
    psum x1, blocking collectives, per_device(): b_part = lax.psum(dot(col_weights, b_panel, ((1,), (1,))), 'col')  8.33 us
  transfers between devices with their start and end apart: 2, of which 1 were waited for; matrix products, arithmetic and copies ran while one was open for 1% of the time, Pallas kernels for 0%

commit v1 on v0

v1 whole, which is shorter than its diff:
```python
import functools

import jax
import jax.numpy as jnp
from jax import lax
from jax.experimental import pallas as pl
from jax.experimental.pallas import tpu as pltpu
from jax.sharding import PartitionSpec as P

MESH = pl.DeviceIdType.MESH
WIDTH = 256
AHEAD = 3


def exact_dot(left, right, dims):
    return lax.dot_general(
        left, right, (dims, ((), ())), precision=lax.Precision.HIGHEST, preferred_element_type=jnp.float32
    )


def split(value):
    high = value.astype(jnp.bfloat16)
    return high, (value - high.astype(jnp.float32)).astype(jnp.bfloat16)


def kernel(
    R, C, a_ref, b_ref, rw_ref, cw_ref, prod, rows_out, cols_out,
    bbuf, obuf, abuf, a_hi, a_lo, chk, rwp, cwp, sa, sb, ga, gb, bchk,
    local_sem, y_send, y_recv, up_send, dn_send, z_recv, a_send, a_recv,
    sa_send, sa_recv, sb_send, sb_recv, ga_send, ga_recv, gb_send, gb_recv,
    o_local, o_send, o_recv, c_send, c_recv,
):
    Z, G = R // 2, C // 2
    r, c = lax.axis_index("row"), lax.axis_index("col")
    z, y = r // 2, lax.rem(r, 2)
    mate = r + 1 - 2 * y
    sib = c + 1 - 2 * lax.rem(c, 2)
    m, kc = a_ref.shape
    kb, n = b_ref.shape
    H = n // 2
    W = WIDTH
    NC = H // W

    def remote(src, dst, ssem, rsem, where):
        return pltpu.make_async_remote_copy(
            src_ref=src, dst_ref=dst, send_sem=ssem, recv_sem=rsem, device_id=where, device_id_type=MESH
        )

    def same(ref, ssem, rsem, where):
        return remote(ref, ref, ssem, rsem, where)

    barrier = pltpu.get_barrier_semaphore()
    row_peers = [lax.rem(r + d, R) for d in range(1, R)]
    col_peers = [lax.rem(c + d, C) for d in range(1, C)]
    for p in row_peers:
        pl.semaphore_signal(barrier, inc=1, device_id={"row": p}, device_id_type=MESH)
    for p in col_peers:
        pl.semaphore_signal(barrier, inc=1, device_id={"col": p}, device_id_type=MESH)
    own = pltpu.make_async_copy(b_ref.at[:, pl.ds(pl.multiple_of(y * H, H), H)], bbuf.at[r], local_sem)
    own.start()
    abuf[0, c] = a_ref[...]
    pl.semaphore_wait(barrier, R - 1 + C - 1)

    def columns(j):
        return pl.ds(pl.multiple_of(j * W, W), W)

    def y_copy(j):
        src = b_ref.at[:, pl.ds(pl.multiple_of((1 - y) * H + j * W, W), W)]
        return remote(src, bbuf.at[r, :, columns(j)], y_send.at[j], y_recv.at[j], {"row": mate})

    def unit(u, j, to, ssem):
        return same(bbuf.at[pl.ds(2 * u, 2), :, columns(j)], ssem.at[u, j], z_recv.at[u, j], {"row": to})

    def up(u, j):
        return unit(u, j, r + 2, up_send)

    def down(u, j):
        return unit(u, j, r - 2, dn_send)

    same_core = [lax.rem(c + 2 * k, C) for k in range(1, G)]
    a_sends = []

    def a_copy(s, cc, t, where):
        copy = remote(abuf.at[s, cc], abuf.at[t, cc], a_send.at[len(a_sends)], a_recv.at[t, cc], where)
        a_sends.append(copy)
        copy.start()

    def a_wait(t, cc):
        remote(abuf.at[t, cc], abuf.at[t, cc], a_send.at[0], a_recv.at[t, cc], {"row": mate}).wait_recv()

    y_copy(0).start()
    a_copy(0, c, 1, {"row": mate})
    for p in same_core:
        a_copy(0, c, 0, {"col": p})
    a_copy(0, c, 0, {"col": sib})

    @pl.loop(1, NC)
    def _(j):
        y_copy(j).start()

    own.wait()

    def send_own(j):
        y_copy(j).wait_recv()

        @pl.when(z < Z - 1)
        def _():
            up(z, j).start()

        @pl.when(z > 0)
        def _():
            down(z, j).start()

    for j in range(AHEAD):
        send_own(j)

    def forward(j):
        @pl.when(j + AHEAD < NC)
        def _():
            send_own(j + AHEAD)

        for d in range(1, Z):
            @pl.when(z - d >= 0)
            def _():
                up(z - d, j).wait_recv()

                @pl.when(z < Z - 1)
                def _():
                    up(z - d, j).start()

            @pl.when(z + d < Z)
            def _():
                down(z + d, j).wait_recv()

                @pl.when(z > 0)
                def _():
                    down(z + d, j).start()

    rwp[...] = jnp.zeros_like(rwp)
    cwp[...] = jnp.zeros_like(cwp)
    rwp[0:2, :] = rw_ref[...]
    cwp[0:2, :] = cw_ref[...]
    sa[r] = exact_dot(rwp[...], a_ref[...], ((1,), (0,)))
    sb[c] = exact_dot(cwp[...], b_ref[...], ((1,), (1,)))

    def spread(buf, slot, peers, axis, ssem, rsem):
        copies = [
            same(buf.at[slot], ssem.at[i], rsem.at[slot], {axis: p}) for i, p in enumerate(peers)
        ]
        for copy in copies:
            copy.start()
        return copies

    def collect(buf, peers, axis, ssem, rsem):
        for p in peers:
            same(buf.at[p], ssem.at[0], rsem.at[p], {axis: p}).wait_recv()

    small = spread(sa, r, row_peers, "row", sa_send, sa_recv)
    small += spread(sb, c, col_peers, "col", sb_send, sb_recv)

    a_wait(1, c)
    for p in same_core:
        a_copy(1, c, 1, {"col": p})
    a_copy(1, c, 1, {"col": sib})

    collect(sa, row_peers, "row", sa_send, sa_recv)
    collect(sb, col_peers, "col", sb_send, sb_recv)
    ga[c] = jnp.sum(sa[...], axis=0)
    gb[r] = jnp.sum(sb[...], axis=0)
    small += spread(ga, c, col_peers, "col", ga_send, ga_recv)
    small += spread(gb, r, row_peers, "row", gb_send, gb_recv)

    forward(0)

    for t in range(2):
        for p in same_core:
            a_wait(t, p)
            a_copy(t, p, t, {"col": sib})
    collect(ga, col_peers, "col", ga_send, ga_recv)
    collect(gb, row_peers, "row", gb_send, gb_recv)

    forward(1)

    for t in range(2):
        for k in range(G):
            a_wait(t, lax.rem(sib + 2 * k, C))
    for i in range(R):
        bchk[:, i * kb:(i + 1) * kb] = gb[i]
    for i in range(C):
        span = slice(i * kc, (i + 1) * kc)
        for t in range(2):
            high, low = split(abuf[t, i])
            a_hi[t * m:(t + 1) * m, span] = high
            a_lo[t * m:(t + 1) * m, span] = low
        high, low = split(jnp.concatenate([ga[i], jnp.zeros_like(ga[i])], axis=0))
        a_hi[2 * m:2 * m + 16, span] = high
        a_lo[2 * m:2 * m + 16, span] = low
    total = jnp.zeros((8, m), jnp.float32)
    for i in range(C):
        total += exact_dot(bchk[:, i * kc:(i + 1) * kc], abuf[0, i], ((1,), (1,)))
    cols_out[...] = total[0:2]

    def out_local(j):
        return pltpu.make_async_copy(
            obuf.at[j, 0:m], prod.at[:, pl.ds(pl.multiple_of(y * H + j * W, W), W)], o_local.at[j]
        )

    def out_remote(j):
        dst = prod.at[:, pl.ds(pl.multiple_of(y * H + j * W, W), W)]
        return remote(obuf.at[j, m:2 * m], dst, o_send.at[j], o_recv.at[j], {"row": mate})

    def dot(left, right):
        return jnp.dot(left, right, preferred_element_type=jnp.float32)

    @pl.loop(0, NC)
    def _(j):
        @pl.when(j >= 2)
        def _():
            forward(j)

        high, low = split(bbuf[:, :, columns(j)].reshape(R * kb, W))
        acc = dot(a_hi[...], high) + dot(a_hi[...], low) + dot(a_lo[...], high)
        obuf[j] = acc[0:2 * m]
        chk[y, :, columns(j)] = acc[2 * m:2 * m + 8]
        out_remote(j).start()
        out_local(j).start()

    last = same(chk.at[y], c_send, c_recv, {"row": mate})
    last.start()

    @pl.loop(0, NC)
    def _(j):
        y_copy(j).wait_send()
        for u in range(Z):
            @pl.when((z < Z - 1) & (u <= z))
            def _():
                up(u, j).wait_send()

            @pl.when((z > 0) & (u >= z))
            def _():
                down(u, j).wait_send()

    for copy in a_sends + small:
        copy.wait_send()
    last.wait()
    rows_out[:, 0:H] = chk[0, 0:2, :]
    rows_out[:, H:2 * H] = chk[1, 0:2, :]

    @pl.loop(0, NC)
    def _(j):
        out_local(j).wait()
        out_remote(j).wait()


def per_device(R, C, a_slab, b_panel, row_weights, col_weights):
    m, kc = a_slab.shape
    kb, n = b_panel.shape
    Z, G, H = R // 2, C // 2, n // 2
    NC = H // WIDTH
    K = R * kb
    f32, bf16 = jnp.float32, jnp.bfloat16
    dma = pltpu.SemaphoreType.DMA
    vmem = pl.BlockSpec(memory_space=pltpu.VMEM)
    scratch = [
        pltpu.VMEM((R, kb, H), f32),
        pltpu.VMEM((NC, 2 * m, WIDTH), f32),
        pltpu.VMEM((2, C, m, kc), f32),
        pltpu.VMEM((2 * m + 16, K), bf16),
        pltpu.VMEM((2 * m + 16, K), bf16),
        pltpu.VMEM((2, 8, H), f32),
        pltpu.VMEM((8, m), f32),
        pltpu.VMEM((8, n), f32),
        pltpu.VMEM((R, 8, kc), f32),
        pltpu.VMEM((C, 8, kb), f32),
        pltpu.VMEM((C, 8, kc), f32),
        pltpu.VMEM((R, 8, kb), f32),
        pltpu.VMEM((8, K), f32),
        dma,
        dma((NC,)), dma((NC,)),
        dma((Z, NC)), dma((Z, NC)), dma((Z, NC)),
        dma((3 + 4 * (G - 1),)), dma((2, C)),
        dma((R,)), dma((R,)), dma((C,)), dma((C,)),
        dma((C,)), dma((C,)), dma((R,)), dma((R,)),
        dma((NC,)), dma((NC,)), dma((NC,)),
        dma, dma,
    ]
    return pl.pallas_call(
        functools.partial(kernel, R, C),
        out_shape=(
            jax.ShapeDtypeStruct((m, n), f32),
            jax.ShapeDtypeStruct((2, n), f32),
            jax.ShapeDtypeStruct((2, m), f32),
        ),
        in_specs=[vmem] * 4,
        out_specs=(pl.BlockSpec(memory_space=pl.ANY), vmem, vmem),
        scratch_shapes=scratch,
        compiler_params=pltpu.CompilerParams(
            collective_id=0, has_side_effects=True, vmem_limit_bytes=56 * 1024 * 1024
        ),
    )(a_slab, b_panel, row_weights, col_weights)


def solution(mesh):
    placed = (P("row", "col"), P("row", "col"), P(None, "row"), P(None, "col"))
    return jax.shard_map(
        functools.partial(per_device, mesh.shape["row"], mesh.shape["col"]),
        mesh=mesh,
        in_specs=placed,
        out_specs=(P("row", "col"), P(None, "col"), P(None, "row")),
        check_vma=False,
    )
```

time: 297 us -> 189 us (0.64)
  waiting for transfers between devices: 201 us -> 0 us
  Pallas kernels: 0 us -> 179 us
  blocking collectives: 51.7 us -> 0 us
  matrix products: 29.3 us -> 0 us
  between operations: 14.1 us -> 0.66 us
  local copies, waits for them, and re-layouts: 0.11 us -> 8.99 us
    all_gather x2 -> x0, waiting for transfers between devices: 200 us -> none  [the longest x1 200 us: per_device(): b_whole = lax.all_gather(b_panel, 'row', axis=0, tiled=True)]
    pallas_call x0 -> x1, Pallas kernels: none -> 179 us  [per_device(): pl.pallas_call(functools.partial(kernel, R, C), out_shape=(jax.ShapeDtype...]
    psum x2 -> x0, blocking collectives: 30 us -> none  [the longest x1 21.7 us: per_device(): a_part = lax.psum(dot(row_weights, a_slab, ((1,), (0,))), 'row')]
    dot_general x5 -> x0, matrix products: 29.3 us -> none  [dot(): lax.dot_general(left, right, (dims, ((), ())), precision=lax.Precision.HI...]
    all_gather x2 -> x0, blocking collectives: 21.6 us -> none  [the longest x1 16.5 us: per_device(): b_check = lax.all_gather(b_part, 'row', axis=1, tiled=True)]
    unnamed x12 -> x7, local copies, waits for them, and re-layouts: 0.11 us -> 8.99 us
  transfers between devices with their start and end apart: 2 -> 0, of which waited for: 1 -> 0; matrix products, arithmetic and copies ran while one was open for 1% -> 0% of each run, Pallas kernels for 0% -> 0%
where the time goes in v1:
time: 189 us
  Pallas kernels  179 us (95%)
  local copies, waits for them, and re-layouts  8.99 us (5%)
    pallas_call x1, Pallas kernels, per_device(): pl.pallas_call(functools.partial(kernel, R, C), out_shape=(jax.ShapeDtype...  179 us
    unnamed x7, local copies, waits for them, and re-layouts  8.99 us

profile of v1, /device:TPU:0, one launch (start us, length us, event | category | flops | bytes accessed | tf_op | source)
XLA Modules:
  0.0 188.9 jit_solution(15116862310381239516)
XLA Ops:
  0.6 179.3 %shard_map.67 = (f32[512,4096]{1,0:T(8,128)}, f32[2,4096]{1,0:T(2,128)}, f32[2,512]{1,0:T(2,128)}) custom-call(f32[512,256]{1,0:T(8,128)} %a_ref.1, f32[128,4096]{1,0:T(8,128)} %b_ref.1, f32[2,512]{1,0:T(2,128)} %rw_ref.1, f32[2,4096]{1,0:T(2,128)} %cw_ref.1), custom_call_target="tpu_custom_call" | custom-call | tf_op jit(solution)/shard_map/pallas_call | solution.py:287
  179.9 0.0 copy-start
  179.9 0.0 copy-start.1
  180.0 7.8 %copy.10 = f32[512,4096]{1,0:T(8,128)} copy(f32[512,4096]{1,0:T(8,128)} %get-tuple-element.6) | data formatting | bytes 16777216
  187.7 0.0 copy-done
  187.7 0.6 copy.11
  188.4 0.0 copy-done.1
  188.4 0.6 copy.12
Async XLA Ops:
  179.9 7.8 %copy-start = (f32[2,4096]{1,0:T(2,128)S(1)}, f32[2,4096]{1,0:T(2,128)}, u32[]{:S(2)}) copy-start(f32[2,4096]{1,0:T(2,128)} %get-tuple-element.7) | copy-start | bytes 98308
  179.9 8.4 %copy-start.1 = (f32[2,512]{1,0:T(2,128)S(1)}, f32[2,512]{1,0:T(2,128)}, u32[]{:S(2)}) copy-start(f32[2,512]{1,0:T(2,128)} %get-tuple-element.8) | copy-start | bytes 12292

commit v2 on v1

--- a/solution.py
+++ b/solution.py
@@ -8,8 +8,9 @@
 from jax.sharding import PartitionSpec as P
 
 MESH = pl.DeviceIdType.MESH
-WIDTH = 256
-AHEAD = 3
+WIDTH = 128
+AHEAD = 6
+PACE = 6
 
 
 def exact_dot(left, right, dims):
@@ -28,7 +29,7 @@
     bbuf, obuf, abuf, a_hi, a_lo, chk, rwp, cwp, sa, sb, ga, gb, bchk,
     local_sem, y_send, y_recv, up_send, dn_send, z_recv, a_send, a_recv,
     sa_send, sa_recv, sb_send, sb_recv, ga_send, ga_recv, gb_send, gb_recv,
-    o_local, o_send, o_recv, c_send, c_recv,
+    o_send, o_recv, c_send, c_recv,
 ):
     Z, G = R // 2, C // 2
     r, c = lax.axis_index("row"), lax.axis_index("col")
@@ -69,7 +70,7 @@
         return remote(src, bbuf.at[r, :, columns(j)], y_send.at[j], y_recv.at[j], {"row": mate})
 
     def unit(u, j, to, ssem):
-        return same(bbuf.at[pl.ds(2 * u, 2), :, columns(j)], ssem.at[u, j], z_recv.at[u, j], {"row": to})
+        return same(bbuf.at[pl.ds(2 * u, 2), :, columns(j)], ssem.at[2 * u, j], z_recv.at[u, j], {"row": to})
 
     def up(u, j):
         return unit(u, j, r + 2, up_send)
@@ -88,36 +89,44 @@
     def a_wait(t, cc):
         remote(abuf.at[t, cc], abuf.at[t, cc], a_send.at[0], a_recv.at[t, cc], {"row": mate}).wait_recv()
 
-    y_copy(0).start()
     a_copy(0, c, 1, {"row": mate})
     for p in same_core:
         a_copy(0, c, 0, {"col": p})
     a_copy(0, c, 0, {"col": sib})
-
-    @pl.loop(1, NC)
+    for j in range(2):
+        y_copy(j).start()
+
+    def own_block(row, j, to, ssem):
+        src = dst = bbuf.at[row, :, columns(j)]
+        if row is r:
+            src = b_ref.at[:, pl.ds(pl.multiple_of(y * H + j * W, W), W)]
+        return remote(src, dst, ssem.at[row, j], z_recv.at[z, j], {"row": to})
+
+    def send_block(row, j):
+        @pl.when(z < Z - 1)
+        def _():
+            own_block(row, j, r + 2, up_send).start()
+
+        @pl.when(z > 0)
+        def _():
+            own_block(row, j, r - 2, dn_send).start()
+
+    @pl.loop(0, NC)
     def _(j):
-        y_copy(j).start()
-
-    own.wait()
-
-    def send_own(j):
+        send_block(r, j)
+
+    def send_mate(j):
         y_copy(j).wait_recv()
-
-        @pl.when(z < Z - 1)
-        def _():
-            up(z, j).start()
-
-        @pl.when(z > 0)
-        def _():
-            down(z, j).start()
-
-    for j in range(AHEAD):
-        send_own(j)
+        send_block(mate, j)
+
+        @pl.when(j + PACE < NC)
+        def _():
+            y_copy(j + PACE).start()
 
     def forward(j):
         @pl.when(j + AHEAD < NC)
         def _():
-            send_own(j + AHEAD)
+            send_mate(j + AHEAD)
 
         for d in range(1, Z):
             @pl.when(z - d >= 0)
@@ -162,6 +171,10 @@
     for p in same_core:
         a_copy(1, c, 1, {"col": p})
     a_copy(1, c, 1, {"col": sib})
+    for j in range(2, PACE):
+        y_copy(j).start()
+    for j in range(3):
+        send_mate(j)
 
     collect(sa, row_peers, "row", sa_send, sa_recv)
     collect(sb, col_peers, "col", sb_send, sb_recv)
@@ -170,7 +183,8 @@
     small += spread(ga, c, col_peers, "col", ga_send, ga_recv)
     small += spread(gb, r, row_peers, "row", gb_send, gb_recv)
 
-    forward(0)
+    for j in range(3, AHEAD):
+        send_mate(j)
 
     for t in range(2):
         for p in same_core:
@@ -179,7 +193,7 @@
     collect(ga, col_peers, "col", ga_send, ga_recv)
     collect(gb, row_peers, "row", gb_send, gb_recv)
 
-    forward(1)
+    forward(0)
 
     for t in range(2):
         for k in range(G):
@@ -195,50 +209,71 @@
         high, low = split(jnp.concatenate([ga[i], jnp.zeros_like(ga[i])], axis=0))
         a_hi[2 * m:2 * m + 16, span] = high
         a_lo[2 * m:2 * m + 16, span] = low
+    def shifted(start, width):
+        return pl.ds(pl.multiple_of(y * H + start, W), width)
+
+    def out_remote(start, width, i):
+        return remote(
+            obuf.at[:, pl.ds(start, width)], prod.at[:, shifted(start, width)],
+            o_send.at[i], o_recv.at[i], {"row": mate},
+        )
+
+    def dot(left, right):
+        return jnp.dot(left, right, preferred_element_type=jnp.float32)
+
+    def multiply(start, width, i):
+        span = pl.ds(start, width)
+        high, low = split(bbuf[:, :, span].reshape(R * kb, width))
+        acc = dot(a_hi[...], high) + dot(a_hi[...], low) + dot(a_lo[...], high)
+        prod[:, shifted(start, width)] = acc[0:m]
+        obuf[:, span] = acc[m:2 * m]
+        chk[y, :, span] = acc[2 * m:2 * m + 8]
+        out_remote(start, width, i).start()
+
+    pairs = NC // 2 - 1
+    own.wait()
+
+    @pl.loop(0, pairs)
+    def _(i):
+        @pl.when(i > 0)
+        def _():
+            forward(2 * i)
+
+        forward(2 * i + 1)
+        multiply(pl.multiple_of(2 * i * W, 2 * W), 2 * W, i)
+
+    for i in range(2):
+        forward(2 * pairs + i)
+        multiply((2 * pairs + i) * W, W, pairs + i)
+
+    last = same(chk.at[y], c_send, c_recv, {"row": mate})
+    last.start()
+
     total = jnp.zeros((8, m), jnp.float32)
     for i in range(C):
         total += exact_dot(bchk[:, i * kc:(i + 1) * kc], abuf[0, i], ((1,), (1,)))
     cols_out[...] = total[0:2]
 
-    def out_local(j):
-        return pltpu.make_async_copy(
-            obuf.at[j, 0:m], prod.at[:, pl.ds(pl.multiple_of(y * H + j * W, W), W)], o_local.at[j]
-        )
-
-    def out_remote(j):
-        dst = prod.at[:, pl.ds(pl.multiple_of(y * H + j * W, W), W)]
-        return remote(obuf.at[j, m:2 * m], dst, o_send.at[j], o_recv.at[j], {"row": mate})
-
-    def dot(left, right):
-        return jnp.dot(left, right, preferred_element_type=jnp.float32)
-
-    @pl.loop(0, NC)
-    def _(j):
-        @pl.when(j >= 2)
-        def _():
-            forward(j)
-
-        high, low = split(bbuf[:, :, columns(j)].reshape(R * kb, W))
-        acc = dot(a_hi[...], high) + dot(a_hi[...], low) + dot(a_lo[...], high)
-        obuf[j] = acc[0:2 * m]
-        chk[y, :, columns(j)] = acc[2 * m:2 * m + 8]
-        out_remote(j).start()
-        out_local(j).start()
-
-    last = same(chk.at[y], c_send, c_recv, {"row": mate})
-    last.start()
-
     @pl.loop(0, NC)
     def _(j):
         y_copy(j).wait_send()
         for u in range(Z):
-            @pl.when((z < Z - 1) & (u <= z))
+            @pl.when((z < Z - 1) & (u < z))
             def _():
                 up(u, j).wait_send()
 
-            @pl.when((z > 0) & (u >= z))
+            @pl.when((z > 0) & (u > z))
             def _():
                 down(u, j).wait_send()
+
+        for row in (r, mate):
+            @pl.when(z < Z - 1)
+            def _():
+                own_block(row, j, r + 2, up_send).wait_send()
+
+            @pl.when(z > 0)
+            def _():
+                own_block(row, j, r - 2, dn_send).wait_send()
 
     for copy in a_sends + small:
         copy.wait_send()
@@ -246,10 +281,12 @@
     rows_out[:, 0:H] = chk[0, 0:2, :]
     rows_out[:, H:2 * H] = chk[1, 0:2, :]
 
-    @pl.loop(0, NC)
-    def _(j):
-        out_local(j).wait()
-        out_remote(j).wait()
+    @pl.loop(0, pairs)
+    def _(i):
+        out_remote(pl.multiple_of(2 * i * W, 2 * W), 2 * W, i).wait()
+
+    for i in range(2):
+        out_remote((2 * pairs + i) * W, W, pairs + i).wait()
 
 
 def per_device(R, C, a_slab, b_panel, row_weights, col_weights):
@@ -263,7 +300,7 @@
     vmem = pl.BlockSpec(memory_space=pltpu.VMEM)
     scratch = [
         pltpu.VMEM((R, kb, H), f32),
-        pltpu.VMEM((NC, 2 * m, WIDTH), f32),
+        pltpu.VMEM((m, H), f32),
         pltpu.VMEM((2, C, m, kc), f32),
         pltpu.VMEM((2 * m + 16, K), bf16),
         pltpu.VMEM((2 * m + 16, K), bf16),
@@ -277,25 +314,25 @@
         pltpu.VMEM((8, K), f32),
         dma,
         dma((NC,)), dma((NC,)),
-        dma((Z, NC)), dma((Z, NC)), dma((Z, NC)),
+        dma((R, NC)), dma((R, NC)), dma((Z, NC)),
         dma((3 + 4 * (G - 1),)), dma((2, C)),
         dma((R,)), dma((R,)), dma((C,)), dma((C,)),
         dma((C,)), dma((C,)), dma((R,)), dma((R,)),
-        dma((NC,)), dma((NC,)), dma((NC,)),
+        dma((NC // 2 + 1,)), dma((NC // 2 + 1,)),
         dma, dma,
     ]
     return pl.pallas_call(
         functools.partial(kernel, R, C),
         out_shape=(
-            jax.ShapeDtypeStruct((m, n), f32),
+            pltpu.VMEM((m, n), f32),
             jax.ShapeDtypeStruct((2, n), f32),
             jax.ShapeDtypeStruct((2, m), f32),
         ),
         in_specs=[vmem] * 4,
-        out_specs=(pl.BlockSpec(memory_space=pl.ANY), vmem, vmem),
+        out_specs=(vmem, vmem, vmem),
         scratch_shapes=scratch,
         compiler_params=pltpu.CompilerParams(
-            collective_id=0, has_side_effects=True, vmem_limit_bytes=56 * 1024 * 1024
+            collective_id=0, has_side_effects=True, vmem_limit_bytes=46 * 1024 * 1024
         ),
     )(a_slab, b_panel, row_weights, col_weights)
 

time: 189 us -> 171 us (0.905)
  Pallas kernels: 179 us -> 166 us
  local copies, waits for them, and re-layouts: 8.99 us -> 4.62 us
    pallas_call x1, Pallas kernels: 179 us -> 166 us  [per_device(): pl.pallas_call(functools.partial(kernel, R, C), out_shape=(pltpu.VMEM((m,...]
    unnamed x7, local copies, waits for them, and re-layouts: 8.99 us -> 4.62 us
where the time goes in v2:
time: 171 us
  Pallas kernels  166 us (97%)
  local copies, waits for them, and re-layouts  4.62 us (3%)
    pallas_call x1, Pallas kernels, per_device(): pl.pallas_call(functools.partial(kernel, R, C), out_shape=(pltpu.VMEM((m,...  166 us
    unnamed x7, local copies, waits for them, and re-layouts  4.62 us

profile of v2, /device:TPU:0, one launch (start us, length us, event | category | flops | bytes accessed | tf_op | source)
XLA Modules:
  0.0 170.8 jit_solution(3722632975055421620)
XLA Ops:
  0.6 165.5 %shard_map.67 = (f32[512,4096]{1,0:T(8,128)S(1)}, f32[2,4096]{1,0:T(2,128)}, f32[2,512]{1,0:T(2,128)}) custom-call(f32[512,256]{1,0:T(8,128)} %a_ref.1, f32[128,4096]{1,0:T(8,128)} %b_ref.1, f32[2,512]{1,0:T(2,128)} %rw_ref.1, f32[2,4096]{1,0:T(2,128)} %cw_ref.1), custom_call_target="tpu_custom_call" | custom-call | tf_op jit(solution)/shard_map/pallas_call | solution.py:324
  166.2 0.0 copy-start
  166.2 0.0 copy-start.1
  166.2 3.4 %copy.10 = f32[512,4096]{1,0:T(8,128)} copy(f32[512,4096]{1,0:T(8,128)S(1)} %get-tuple-element.3) | data formatting | bytes 16777216
  169.6 0.0 copy-done
  169.6 0.6 copy.11
  170.2 0.0 copy-done.1
  170.2 0.6 copy.12
Async XLA Ops:
  166.2 3.4 %copy-start = (f32[2,4096]{1,0:T(2,128)S(1)}, f32[2,4096]{1,0:T(2,128)}, u32[]{:S(2)}) copy-start(f32[2,4096]{1,0:T(2,128)} %get-tuple-element.10) | copy-start | bytes 98308
  166.2 4.0 %copy-start.1 = (f32[2,512]{1,0:T(2,128)S(1)}, f32[2,512]{1,0:T(2,128)}, u32[]{:S(2)}) copy-start(f32[2,512]{1,0:T(2,128)} %get-tuple-element.11) | copy-start | bytes 12292

commit v3 on v2

--- a/solution.py
+++ b/solution.py
@@ -11,6 +11,7 @@
 WIDTH = 128
 AHEAD = 6
 PACE = 6
+TAIL = 8
 
 
 def exact_dot(left, right, dims):
@@ -230,7 +231,7 @@
         chk[y, :, span] = acc[2 * m:2 * m + 8]
         out_remote(start, width, i).start()
 
-    pairs = NC // 2 - 1
+    pairs = (NC - TAIL) // 2
     own.wait()
 
     @pl.loop(0, pairs)
@@ -242,17 +243,23 @@
         forward(2 * i + 1)
         multiply(pl.multiple_of(2 * i * W, 2 * W), 2 * W, i)
 
-    for i in range(2):
-        forward(2 * pairs + i)
-        multiply((2 * pairs + i) * W, W, pairs + i)
-
-    last = same(chk.at[y], c_send, c_recv, {"row": mate})
-    last.start()
-
+    def rows_copy(start, width, i):
+        return same(chk.at[y, :, pl.ds(start, width)], c_send.at[i], c_recv.at[i], {"row": mate})
+
+    bulk = rows_copy(0, 2 * pairs * W, 0)
+    bulk.start()
     total = jnp.zeros((8, m), jnp.float32)
     for i in range(C):
         total += exact_dot(bchk[:, i * kc:(i + 1) * kc], abuf[0, i], ((1,), (1,)))
     cols_out[...] = total[0:2]
+
+    @pl.loop(0, TAIL)
+    def _(i):
+        forward(2 * pairs + i)
+        multiply(pl.multiple_of((2 * pairs + i) * W, W), W, pairs + i)
+
+    last = rows_copy(2 * pairs * W, TAIL * W, 1)
+    last.start()
 
     @pl.loop(0, NC)
     def _(j):
@@ -277,6 +284,7 @@
 
     for copy in a_sends + small:
         copy.wait_send()
+    bulk.wait()
     last.wait()
     rows_out[:, 0:H] = chk[0, 0:2, :]
     rows_out[:, H:2 * H] = chk[1, 0:2, :]
@@ -285,8 +293,9 @@
     def _(i):
         out_remote(pl.multiple_of(2 * i * W, 2 * W), 2 * W, i).wait()
 
-    for i in range(2):
-        out_remote((2 * pairs + i) * W, W, pairs + i).wait()
+    @pl.loop(0, TAIL)
+    def _(i):
+        out_remote(pl.multiple_of((2 * pairs + i) * W, W), W, pairs + i).wait()
 
 
 def per_device(R, C, a_slab, b_panel, row_weights, col_weights):
@@ -318,15 +327,15 @@
         dma((3 + 4 * (G - 1),)), dma((2, C)),
         dma((R,)), dma((R,)), dma((C,)), dma((C,)),
         dma((C,)), dma((C,)), dma((R,)), dma((R,)),
-        dma((NC // 2 + 1,)), dma((NC // 2 + 1,)),
-        dma, dma,
+        dma(((NC + TAIL) // 2,)), dma(((NC + TAIL) // 2,)),
+        dma((2,)), dma((2,)),
     ]
     return pl.pallas_call(
         functools.partial(kernel, R, C),
         out_shape=(
             pltpu.VMEM((m, n), f32),
-            jax.ShapeDtypeStruct((2, n), f32),
-            jax.ShapeDtypeStruct((2, m), f32),
+            pltpu.VMEM((2, n), f32),
+            pltpu.VMEM((2, m), f32),
         ),
         in_specs=[vmem] * 4,
         out_specs=(vmem, vmem, vmem),

time: 171 us -> 168 us (0.982)
  Pallas kernels: 166 us -> 162 us
    pallas_call x1, Pallas kernels: 166 us -> 162 us  [per_device(): pl.pallas_call(functools.partial(kernel, R, C), out_shape=(pltpu.VMEM((m,...]
    unnamed x7 -> x3, local copies, waits for them, and re-layouts: 4.62 us -> 4.61 us
where the time goes in v3:
time: 168 us; the launch traced here: 167 us
  Pallas kernels  162 us (96%)
  local copies, waits for them, and re-layouts  4.61 us (3%)
    pallas_call x1, Pallas kernels, per_device(): pl.pallas_call(functools.partial(kernel, R, C), out_shape=(pltpu.VMEM((m,...  162 us
    unnamed x3, local copies, waits for them, and re-layouts  4.61 us

profile of v3, /device:TPU:0, one launch (start us, length us, event | category | flops | bytes accessed | tf_op | source)
XLA Modules:
  0.0 167.4 jit_solution(826468822357806883)
XLA Ops:
  0.6 162.2 %shard_map.67 = (f32[512,4096]{1,0:T(8,128)S(1)}, f32[2,4096]{1,0:T(2,128)S(1)}, f32[2,512]{1,0:T(2,128)S(1)}) custom-call(f32[512,256]{1,0:T(8,128)} %a_ref.1, f32[128,4096]{1,0:T(8,128)} %b_ref.1, f32[2,512]{1,0:T(2,128)} %rw_ref.1, f32[2,4096]{1,0:T(2,128)} %cw_ref.1), custom_call_target="tpu_custom_call" | custom-call | tf_op jit(solution)/shard_map/pallas_call | solution.py:333
  162.8 3.4 %copy.10 = f32[512,4096]{1,0:T(8,128)} copy(f32[512,4096]{1,0:T(8,128)S(1)} %get-tuple-element.3) | data formatting | bytes 16777216
  166.2 0.6 copy.12
  166.8 0.6 copy.11
